TPU v7x, 32 devices: a whole 2x2x4 slice. The times are simulated.
32 devices in a mesh: rows: 4 (over z), nodes: 8 (over y, x, core).
Axes of the slice: x: 2, y: 2, z: 4, core: 2. Of those that a mesh axis runs over, the one named last changes fastest.
Arguments:
- codes: int32 [65536, 128], P('rows'), may hold values from 0 to 16367
- sample_idx: int32 [32768], P(('rows', 'nodes')), may hold values from 0 to 16383, as said below
- node_of_row: int32 [32768, 1], P(('rows', 'nodes')), may hold values from 0 to 63; in each aligned block of 1024 rows (0 to 1023, 1024 to 2047, ...) at most 48 rows name the same one
- small_flag: int32 [32768], P(('rows', 'nodes')), may hold values 0 or 1
- preds: bfloat16 [16, 32768], P(None, ('rows', 'nodes')), may hold values from -6 to 6
- targets: float32 [32768], P(('rows', 'nodes')), may hold values from -6 to 6
Outputs:
- best_gain: float32 [64, 256], P('nodes', 'rows')
Inputs may be any that keep to these rules, and one draw needn't show every extreme that they name: `node_of_row`: in each aligned block of 1024 rows (the rows of one device) no node is named by more than 48 rows, a bound that some block reaches. `sample_idx`: distinct within each aligned block of 8192 rows.
All inputs are finite; a program needn't handle non-finite values. No bound on the sum of `small_flag` on one device may be relied on, other than what follows from the above.
Results may differ from a plain program's by a relative error of at most 0.00099.
Values may be sent and summed in bfloat16 or wider, within the bound.
A program may use at most 128 MiB of HBM per device.

v0:
```python
import functools
import math

import jax
import jax.numpy as jnp
from jax import lax
from jax.experimental import pallas as pl
from jax.experimental.pallas import tpu as pltpu
from jax.sharding import PartitionSpec as P

BINS = 128
CAP = 48
TOTAL_NODES = 64
SMOOTH = 0.5
RIDGE = 1.0
BOOST = 8.0
CHANS = 32
TILE = 128
STEP = 8
PART = 256
ALIGN = 16
VMEM = pl.BlockSpec(memory_space=pltpu.VMEM)
SMEM = pl.BlockSpec(memory_space=pltpu.SMEM)


def send_kernel(preds_ref, targets_ref, flag_ref, node_ref, line_ref, out_ref):
    quant, rows = preds_ref.shape
    spread, total, _ = out_ref.shape
    share = line_ref.shape[1] // spread
    levels = (lax.broadcasted_iota(jnp.int32, (quant, 1), 0).astype(jnp.float32) + 0.5) / quant
    weight = 1.0 + (BOOST - 1.0) * flag_ref[...].astype(jnp.float32)
    gap = (preds_ref[...].astype(jnp.float32) - targets_ref[...]) / SMOOTH
    slopes = (1.0 / (1.0 + jnp.exp(-gap)) - levels) * weight
    vals = jnp.concatenate(
        [slopes, weight, node_ref[...].astype(jnp.float32), jnp.zeros((CHANS - quant - 2, rows), jnp.float32)], axis=0
    )
    words = line_ref[...].T
    for z in range(spread):
        word = words[z * share:(z + 1) * share]
        parts = [vals, (word & (BINS - 1)).astype(jnp.float32), (word >> 7).astype(jnp.float32)]
        if total > CHANS + 2 * share:
            parts.append(jnp.zeros((total - CHANS - 2 * share, rows), jnp.float32))
        out_ref[z] = jnp.concatenate(parts, axis=0).astype(jnp.bfloat16)


def pack_kernel(quant, slots, base_ref, size_ref, got_ref, out_ref, upto_ref, acc_ref):
    spread, _, rows = got_ref.shape
    groups = out_ref.shape[0]
    node_grp = TOTAL_NODES // groups
    upto_ref[...] = (
        lax.broadcasted_iota(jnp.int32, (rows, rows), 0) <= lax.broadcasted_iota(jnp.int32, (rows, rows), 1)
    ).astype(jnp.float32).astype(jnp.bfloat16)
    acc_ref[...] = jnp.zeros_like(acc_ref)
    slot = lax.broadcasted_iota(jnp.int32, (PART, rows), 0)

    def block(z, carry):
        vals = got_ref[z].astype(jnp.float32)
        group = vals[quant + 1:quant + 2].astype(jnp.int32) // node_grp
        vals = vals.T.astype(jnp.bfloat16)
        own = (lax.broadcasted_iota(jnp.int32, (groups, rows), 0) == group).astype(jnp.float32)
        run = jnp.dot(own.astype(jnp.bfloat16), upto_ref[...], preferred_element_type=jnp.float32)
        rank = jnp.sum(run * own, axis=0, keepdims=True).astype(jnp.int32) - 1

        def put(g, at):
            base = base_ref[z * groups + g]
            start = base // ALIGN * ALIGN
            pick = slot == jnp.where(group == g, rank + (base - start - at), -1)
            pick = pick.astype(jnp.float32).astype(jnp.bfloat16)
            window = pl.ds(pl.multiple_of(start + at, ALIGN), PART)
            added = jnp.dot(pick, vals, preferred_element_type=jnp.float32)
            acc_ref[g, window, :] = (acc_ref[g, window, :].astype(jnp.float32) + added).astype(jnp.bfloat16)

        for g in range(groups):
            put(g, 0)
        for g in range(groups):
            for at in range(PART, slots + ALIGN, PART):
                pl.when(base_ref[z * groups + g] % ALIGN + size_ref[z * groups + g] > at)(functools.partial(put, g, at))
        return carry

    lax.fori_loop(0, spread, block, 0)

    def turn(c, carry):
        window = pl.ds(pl.multiple_of(c * slots, TILE), slots)
        for g in range(groups):
            out_ref[g, :, window] = acc_ref[g, window, :].astype(jnp.float32).T.astype(jnp.bfloat16)
        return carry

    lax.fori_loop(0, spread, turn, 0)


def gain_kernel(quant, count_ref, chan_ref, out_ref, list_ref, left_ref, tile_ref, acc_ref):
    groups, _, slots = chan_ref.shape
    node_grp, words = out_ref.shape[0], out_ref.shape[1] // 2
    per = slots // TILE

    def fill(src, used):
        tiles = (count_ref[src] + TILE - 1) // TILE

        def put(s, used):
            list_ref[used] = src * per + s
            return used + 1

        return lax.fori_loop(0, tiles, put, used)

    used = lax.fori_loop(0, groups, fill, jnp.int32(0))
    for u in range(STEP):
        list_ref[used + u] = -1
    acc_ref[...] = jnp.zeros_like(acc_ref)
    kinds = lax.broadcasted_iota(jnp.int32, (node_grp, TILE), 0)
    level = lax.broadcasted_iota(jnp.int32, (BINS, STEP * TILE), 0).astype(jnp.float32).astype(jnp.bfloat16)

    def step(j, carry):
        for u in range(STEP):
            entry = list_ref[j * STEP + u]
            tile = jnp.maximum(entry, 0)
            src = tile // per
            at = pl.ds(pl.multiple_of(tile % per * TILE, TILE), TILE)
            part = chan_ref[src, 0:CHANS, at].astype(jnp.float32)
            kind = jnp.bitwise_and(part[quant + 1:quant + 2].astype(jnp.int32), node_grp - 1)
            mask = jnp.where((kind == kinds) & (entry >= 0), 1.0, 0.0)
            for c in range(quant + 1):
                left_ref[c * node_grp:(c + 1) * node_grp, u * TILE:(u + 1) * TILE] = part[c:c + 1] * mask
            tile_ref[u] = chan_ref[src, CHANS:, at].astype(jnp.float32)
        left = left_ref[...].T.astype(jnp.bfloat16)

        def feature(w, carry):
            sides = []
            for at in (w, words + w):
                digit = jnp.concatenate([tile_ref[u, pl.ds(at, 1), :] for u in range(STEP)], axis=1)
                digit = jnp.broadcast_to(digit, (16, STEP * TILE)).astype(jnp.bfloat16)
                digit = jnp.broadcast_to(digit[None], (BINS // 16, 16, STEP * TILE)).reshape(BINS, STEP * TILE)
                sides.append(jnp.where(level >= digit, jnp.bfloat16(1), jnp.bfloat16(0)))
            side = jnp.concatenate(sides, axis=0)
            acc_ref[w] += jnp.dot(side, left, preferred_element_type=jnp.float32)
            return carry

        return lax.fori_loop(0, words, feature, carry, unroll=math.gcd(words, 16))

    lax.fori_loop(0, (used + STEP - 1) // STEP, step, 0)

    lane = lax.broadcasted_iota(jnp.int32, out_ref.shape, 1)
    bins = lax.broadcasted_iota(jnp.int32, (node_grp, BINS), 1)

    def best_of(w, best):
        for c in range(2):
            sums = acc_ref[w, c * BINS:(c + 1) * BINS, :].T
            hess = sums[quant * node_grp:]
            hess_all = hess[:, BINS - 1:]
            sq_left = sq_right = sq_all = 0.0
            for q in range(quant):
                grad = sums[q * node_grp:(q + 1) * node_grp]
                grad_all = grad[:, BINS - 1:]
                sq_left += grad * grad
                sq_right += (grad_all - grad) * (grad_all - grad)
                sq_all += grad_all * grad_all
            score = sq_left / (hess + RIDGE) + sq_right / (hess_all - hess + RIDGE) - sq_all / (hess_all + RIDGE)
            score = jnp.where(bins < BINS - 1, score, -jnp.inf)
            top = jnp.max(score, axis=1, keepdims=True) / quant
            best = jnp.where(lane == 2 * w + c, top, best)
        return best

    out_ref[...] = lax.fori_loop(0, words, best_of, jnp.zeros(out_ref.shape, jnp.float32), unroll=math.gcd(words, 4))


def on_device(codes, sample_idx, node_of_row, small_flag, preds, targets):
    groups = lax.axis_size("nodes")
    spread = lax.axis_size("rows")
    quant, rows = preds.shape
    node_grp = TOTAL_NODES // groups
    slots = CAP * node_grp
    width = spread * slots
    share = codes.shape[1] // spread
    digits = -(-2 * share // 16) * 16
    total = CHANS + digits

    def line(x):
        return x.reshape(1, rows)

    lines = codes.at[sample_idx].get(mode="promise_in_bounds")
    ready = pl.pallas_call(
        send_kernel,
        out_shape=jax.ShapeDtypeStruct((spread, total, rows), jnp.bfloat16),
        in_specs=[VMEM] * 5,
        out_specs=VMEM,
        compiler_params=pltpu.CompilerParams(vmem_limit_bytes=40 << 20),
    )(preds, line(targets), line(small_flag), line(node_of_row), lines)
    blocks = lax.all_to_all(ready, "rows", split_axis=0, concat_axis=0, tiled=True)
    group = blocks[:, quant + 1, :].astype(jnp.int32) // node_grp
    sizes = jnp.sum((group[:, None, :] == jnp.arange(groups, dtype=jnp.int32)[None, :, None]).astype(jnp.int32), axis=-1)
    before = jnp.arange(spread)[:, None] > jnp.arange(spread)[None, :]
    base = jnp.sum(jnp.where(before[:, :, None], sizes[None], 0), axis=1).reshape(-1)
    packed = pl.pallas_call(
        functools.partial(pack_kernel, quant, slots),
        out_shape=jax.ShapeDtypeStruct((groups, total, width), jnp.bfloat16),
        in_specs=[SMEM, SMEM, VMEM],
        out_specs=VMEM,
        scratch_shapes=[
            pltpu.VMEM((rows, rows), jnp.bfloat16),
            pltpu.VMEM((groups, width + 2 * PART, total), jnp.bfloat16),
        ],
        compiler_params=pltpu.CompilerParams(vmem_limit_bytes=58 << 20),
    )(base, sizes.reshape(-1), blocks)
    got = lax.all_to_all(packed, "nodes", split_axis=0, concat_axis=0, tiled=True)
    count = jnp.sum((got[:, quant, :] > 0).astype(jnp.int32), axis=-1)
    return pl.pallas_call(
        functools.partial(gain_kernel, quant),
        out_shape=jax.ShapeDtypeStruct((node_grp, 2 * share), jnp.float32),
        in_specs=[SMEM, VMEM],
        out_specs=VMEM,
        scratch_shapes=[
            pltpu.SMEM((groups * width // TILE + 2 * STEP,), jnp.int32),
            pltpu.VMEM(((quant + 1) * node_grp, STEP * TILE), jnp.float32),
            pltpu.VMEM((STEP, digits, TILE), jnp.float32),
            pltpu.VMEM((share, 2 * BINS, (quant + 1) * node_grp), jnp.float32),
        ],
        compiler_params=pltpu.CompilerParams(vmem_limit_bytes=48 << 20),
    )(count, got)


def solution(mesh):
    return jax.shard_map(
        on_device,
        mesh=mesh,
        in_specs=(
            P("rows", None),
            P(("rows", "nodes")),
            P(("rows", "nodes"), None),
            P(("rows", "nodes")),
            P(None, ("rows", "nodes")),
            P(("rows", "nodes")),
        ),
        out_specs=P("nodes", "rows"),
        check_vma=False,
    )
```

profile of v0, /device:TPU:2, one launch (start us, length us, event | category | flops | bytes accessed | tf_op | source)
XLA Modules:
  0.0 118.3 jit_solution(16068362735963551164)
XLA Ops:
  0.0 0.7 fusion.1
  0.7 0.0 copy-start
  0.7 0.0 copy-start.1
  0.7 0.0 copy-start.2
  0.7 0.0 copy-start.3
  0.7 6.2 %gather_fusion = s32[1024,128]{1,0:T(8,128)S(1)} fusion(s32[16384,128]{1,0:T(8,128)} %param.6, s32[1024]{0:T(1024)S(1)} %fusion.1), kind=kCustom, calls=%fused_computation | custom fusion | bytes 1052672 | tf_op jit(solution)/shard_map/gather | solution.py:179
  6.9 0.0 copy-done
  7.0 0.0 copy-done.1
  7.0 0.0 copy-done.2
  7.0 0.0 copy-done.3
  7.0 1.1 shard_map.64
  8.1 4.9 %all-to-all-start = ((bf16[4,96,1024]{2,1,0:T(8,128)(2,1)}), bf16[4,96,1024]{2,1,0:T(8,128)(2,1)S(1)}, u32[]{:S(2)}, u32[]{:S(2)}) async-start(bf16[4,96,1024]{2,1,0:T(8,128)(2,1)} %shard_map.64), calls=%async_computation | async-start | bytes 1572864 | tf_op jit(solution)/shard_map/all_to_all | solution.py:187
  13.0 20.1 %all-to-all-done.got_ref = bf16[4,96,1024]{2,1,0:T(8,128)(2,1)S(1)} async-done(((bf16[4,96,1024]{2,1,0:T(8,128)(2,1)}), bf16[4,96,1024]{2,1,0:T(8,128)(2,1)S(1)}, u32[]{:S(2)}, u32[]{:S(2)}) %all-to-all-start) | async-done | bytes 786464 | tf_op jit(solution)/shard_map/all_to_all | solution.py:187
  33.1 0.0 copy-start.4
  33.1 0.1 and_select_fusion
  33.2 0.2 convert_reduce_fusion
  33.3 0.6 reshape.35.size_ref
  33.9 0.1 select_reduce_fusion
  34.0 0.6 reshape.34.base_ref
  34.6 0.0 copy-done.4
  34.6 11.1 %shard_map.65 = bf16[8,96,1536]{2,1,0:T(8,128)(2,1)} custom-call(s32[32]{0:T(128)} %reshape.34.base_ref, s32[32]{0:T(128)} %reshape.35.size_ref, bf16[4,96,1024]{2,1,0:T(8,128)(2,1)} %copy-done.4), custom_call_target="tpu_custom_call" | custom-call | tf_op jit(solution)/shard_map/pallas_call | solution.py:192
  45.7 32.2 %all_to_all.10.chan_ref = bf16[8,96,1536]{2,1,0:T(8,128)(2,1)S(1)} all-to-all(bf16[8,96,1536]{2,1,0:T(8,128)(2,1)} %shard_map.65), channel_id=1, replica_groups=mesh['rows'=4,'nodes'=8] {'nodes'}, dimensions={0} | all-to-all | bytes 4718592 | tf_op jit(solution)/shard_map/all_to_all | solution.py:203
  77.9 0.3 fusion.count_ref
  78.2 40.1 %shard_map.66 = f32[8,64]{1,0:T(8,128)} custom-call(s32[8]{0:T(128)S(1)} %fusion.count_ref, bf16[8,96,1536]{2,1,0:T(8,128)(2,1)S(1)} %all_to_all.10.chan_ref), custom_call_target="tpu_custom_call" | custom-call | tf_op jit(solution)/shard_map/pallas_call | solution.py:205
  (2 shorter events, 0.0 us)
Async XLA Ops:
  0.7 6.3 %copy-start = (bf16[16,1024]{1,0:T(8,128)(2,1)S(1)}, bf16[16,1024]{1,0:T(8,128)(2,1)}, u32[]{:S(2)}) copy-start(bf16[16,1024]{1,0:T(8,128)(2,1)} %preds_ref.1) | copy-start | bytes 98308
  0.7 6.3 %copy-start.1 = (f32[1024]{0:T(1024)S(1)}, f32[1024]{0:T(1024)}, u32[]{:S(2)}) copy-start(f32[1024]{0:T(1024)} %param.11) | copy-start | bytes 12292
  0.7 6.3 %copy-start.2 = (s32[1024]{0:T(1024)S(1)}, s32[1024]{0:T(1024)}, u32[]{:S(2)}) copy-start(s32[1024]{0:T(1024)} %param.9) | copy-start | bytes 12292
  0.7 6.3 %copy-start.3 = (s32[1024,1]{0,1:T(1,128)S(1)}, s32[1024,1]{0,1:T(1,128)}, u32[]{:S(2)}) copy-start(s32[1024,1]{0,1:T(1,128)} %param.8) | copy-start | bytes 12292
  8.1 25.0 %all-to-all-start = ((bf16[4,96,1024]{2,1,0:T(8,128)(2,1)}), bf16[4,96,1024]{2,1,0:T(8,128)(2,1)S(1)}, u32[]{:S(2)}, u32[]{:S(2)}) async-start(bf16[4,96,1024]{2,1,0:T(8,128)(2,1)} %shard_map.64), calls=%async_computation | async-start | bytes 1572864 | tf_op jit(solution)/shard_map/all_to_all | solution.py:187
  33.1 1.5 %copy-start.4 = (bf16[4,96,1024]{2,1,0:T(8,128)(2,1)}, bf16[4,96,1024]{2,1,0:T(8,128)(2,1)S(1)}, u32[]{:S(2)}) copy-start(bf16[4,96,1024]{2,1,0:T(8,128)(2,1)S(1)} %all-to-all-done.got_ref) | copy-start | bytes 2359300
where the time goes:
time: 119 us; the launch traced here: 118 us
  Pallas kernels  52.3 us (44%)
  blocking collectives  32.2 us (27%)
  waiting for transfers between devices  20.1 us (17%)
  local copies, waits for them, and re-layouts  7.42 us (6%)
  starting transfers between devices  4.87 us (4%)
  other arithmetic  1.29 us (1%)
    pallas_call x1, Pallas kernels, on_device(): pl.pallas_call(functools.partial(gain_kernel, quant), out_shape=jax.Shape...  40.1 us
    all_to_all x1, blocking collectives, on_device(): lax.all_to_all(packed, 'nodes', split_axis=0, concat_axis=0, tiled=True)  32.2 us
    all_to_all x1, waiting for transfers between devices, on_device(): lax.all_to_all(ready, 'rows', split_axis=0, concat_axis=0, tiled=True)  20.1 us
    pallas_call x1, Pallas kernels, on_device(): pl.pallas_call(functools.partial(pack_kernel, quant, slots), out_shape=ja...  11.1 us
    gather x1, local copies, waits for them, and re-layouts, on_device(): lines = codes.at[sample_idx].get(mode='promise_in_bounds')  6.22 us
    all_to_all x1, starting transfers between devices, on_device(): lax.all_to_all(ready, 'rows', split_axis=0, concat_axis=0, tiled=True)  4.87 us
  transfers between devices with their start and end apart: 1, of which 1 were waited for; matrix products, arithmetic and copies ran while one was open for 0% of the time, Pallas kernels for 0%

commit v1 on v0

--- a/solution.py
+++ b/solution.py
@@ -77,7 +77,7 @@
                 pl.when(base_ref[z * groups + g] % ALIGN + size_ref[z * groups + g] > at)(functools.partial(put, g, at))
         return carry
 
-    lax.fori_loop(0, spread, block, 0)
+    lax.fori_loop(0, spread, block, 0, unroll=2 - spread % 2)
 
     def turn(c, carry):
         window = pl.ds(pl.multiple_of(c * slots, TILE), slots)

time: 119 us -> 120 us (level)
  the two profiles are of different devices: /device:TPU:2 before, /device:TPU:1 now
where the time goes in v1:
time: 120 us; the launch traced here: 119 us
  Pallas kernels  52.3 us (44%)
  blocking collectives  33.3 us (28%)
  waiting for transfers between devices  19.6 us (16%)
  local copies, waits for them, and re-layouts  7.42 us (6%)
  starting transfers between devices  5.42 us (5%)
  other arithmetic  1.29 us (1%)
    pallas_call x1, Pallas kernels, on_device(): pl.pallas_call(functools.partial(gain_kernel, quant), out_shape=jax.Shape...  40.1 us
    all_to_all x1, blocking collectives, on_device(): lax.all_to_all(packed, 'nodes', split_axis=0, concat_axis=0, tiled=True)  33.3 us
    all_to_all x1, waiting for transfers between devices, on_device(): lax.all_to_all(ready, 'rows', split_axis=0, concat_axis=0, tiled=True)  19.6 us
    pallas_call x1, Pallas kernels, on_device(): pl.pallas_call(functools.partial(pack_kernel, quant, slots), out_shape=ja...  11.1 us
    gather x1, local copies, waits for them, and re-layouts, on_device(): lines = codes.at[sample_idx].get(mode='promise_in_bounds')  6.22 us
    all_to_all x1, starting transfers between devices, on_device(): lax.all_to_all(ready, 'rows', split_axis=0, concat_axis=0, tiled=True)  5.42 us
  transfers between devices with their start and end apart: 1, of which 1 were waited for; matrix products, arithmetic and copies ran while one was open for 0% of the time, Pallas kernels for 0%

profile of v1, /device:TPU:1, one launch (start us, length us, event | category | flops | bytes accessed | tf_op | source)
XLA Modules:
  0.0 119.4 jit_solution(226120287692375982)
XLA Ops:
  0.0 0.7 fusion.1
  0.7 0.0 copy-start
  0.7 0.0 copy-start.1
  0.7 0.0 copy-start.2
  0.7 0.0 copy-start.3
  0.7 6.2 %gather_fusion = s32[1024,128]{1,0:T(8,128)S(1)} fusion(s32[16384,128]{1,0:T(8,128)} %param.6, s32[1024]{0:T(1024)S(1)} %fusion.1), kind=kCustom, calls=%fused_computation | custom fusion | bytes 1052672 | tf_op jit(solution)/shard_map/gather | solution.py:179
  6.9 0.0 copy-done
  7.0 0.0 copy-done.1
  7.0 0.0 copy-done.2
  7.0 0.0 copy-done.3
  7.0 1.1 shard_map.64
  8.1 5.4 %all-to-all-start = ((bf16[4,96,1024]{2,1,0:T(8,128)(2,1)}), bf16[4,96,1024]{2,1,0:T(8,128)(2,1)S(1)}, u32[]{:S(2)}, u32[]{:S(2)}) async-start(bf16[4,96,1024]{2,1,0:T(8,128)(2,1)} %shard_map.64), calls=%async_computation | async-start | bytes 1572864 | tf_op jit(solution)/shard_map/all_to_all | solution.py:187
  13.5 19.6 %all-to-all-done.got_ref = bf16[4,96,1024]{2,1,0:T(8,128)(2,1)S(1)} async-done(((bf16[4,96,1024]{2,1,0:T(8,128)(2,1)}), bf16[4,96,1024]{2,1,0:T(8,128)(2,1)S(1)}, u32[]{:S(2)}, u32[]{:S(2)}) %all-to-all-start) | async-done | bytes 786464 | tf_op jit(solution)/shard_map/all_to_all | solution.py:187
  33.1 0.0 copy-start.4
  33.1 0.1 and_select_fusion
  33.2 0.2 convert_reduce_fusion
  33.4 0.6 reshape.35.size_ref
  34.0 0.1 select_reduce_fusion
  34.0 0.6 reshape.34.base_ref
  34.6 0.0 copy-done.4
  34.6 11.1 %shard_map.65 = bf16[8,96,1536]{2,1,0:T(8,128)(2,1)} custom-call(s32[32]{0:T(128)} %reshape.34.base_ref, s32[32]{0:T(128)} %reshape.35.size_ref, bf16[4,96,1024]{2,1,0:T(8,128)(2,1)} %copy-done.4), custom_call_target="tpu_custom_call" | custom-call | tf_op jit(solution)/shard_map/pallas_call | solution.py:192
  45.8 33.3 %all_to_all.10.chan_ref = bf16[8,96,1536]{2,1,0:T(8,128)(2,1)S(1)} all-to-all(bf16[8,96,1536]{2,1,0:T(8,128)(2,1)} %shard_map.65), channel_id=1, replica_groups=mesh['rows'=4,'nodes'=8] {'nodes'}, dimensions={0} | all-to-all | bytes 4718592 | tf_op jit(solution)/shard_map/all_to_all | solution.py:203
  79.0 0.3 fusion.count_ref
  79.3 40.1 %shard_map.66 = f32[8,64]{1,0:T(8,128)} custom-call(s32[8]{0:T(128)S(1)} %fusion.count_ref, bf16[8,96,1536]{2,1,0:T(8,128)(2,1)S(1)} %all_to_all.10.chan_ref), custom_call_target="tpu_custom_call" | custom-call | tf_op jit(solution)/shard_map/pallas_call | solution.py:205
  (2 shorter events, 0.0 us)
Async XLA Ops:
  0.7 6.3 %copy-start = (bf16[16,1024]{1,0:T(8,128)(2,1)S(1)}, bf16[16,1024]{1,0:T(8,128)(2,1)}, u32[]{:S(2)}) copy-start(bf16[16,1024]{1,0:T(8,128)(2,1)} %preds_ref.1) | copy-start | bytes 98308
  0.7 6.3 %copy-start.1 = (f32[1024]{0:T(1024)S(1)}, f32[1024]{0:T(1024)}, u32[]{:S(2)}) copy-start(f32[1024]{0:T(1024)} %param.11) | copy-start | bytes 12292
  0.7 6.3 %copy-start.2 = (s32[1024]{0:T(1024)S(1)}, s32[1024]{0:T(1024)}, u32[]{:S(2)}) copy-start(s32[1024]{0:T(1024)} %param.9) | copy-start | bytes 12292
  0.7 6.3 %copy-start.3 = (s32[1024,1]{0,1:T(1,128)S(1)}, s32[1024,1]{0,1:T(1,128)}, u32[]{:S(2)}) copy-start(s32[1024,1]{0,1:T(1,128)} %param.8) | copy-start | bytes 12292
  8.1 25.0 %all-to-all-start = ((bf16[4,96,1024]{2,1,0:T(8,128)(2,1)}), bf16[4,96,1024]{2,1,0:T(8,128)(2,1)S(1)}, u32[]{:S(2)}, u32[]{:S(2)}) async-start(bf16[4,96,1024]{2,1,0:T(8,128)(2,1)} %shard_map.64), calls=%async_computation | async-start | bytes 1572864 | tf_op jit(solution)/shard_map/all_to_all | solution.py:187
  33.1 1.5 %copy-start.4 = (bf16[4,96,1024]{2,1,0:T(8,128)(2,1)}, bf16[4,96,1024]{2,1,0:T(8,128)(2,1)S(1)}, u32[]{:S(2)}) copy-start(bf16[4,96,1024]{2,1,0:T(8,128)(2,1)S(1)} %all-to-all-done.got_ref) | copy-start | bytes 2359300
